TPU v7x, 32 devices: a whole 2x2x4 slice. The times are simulated.
32 devices in a mesh: grp: 1, node: 2 (over core), local: 16 (over z, y, x).
Axes of the slice: x: 2, y: 2, z: 4, core: 2. Of those that a mesh axis runs over, the one named last changes fastest.
Arguments:
- tokens: bfloat16 [2048, 7168], P(('grp', 'node', 'local')), may hold values from -6 to 6
- expert_ids: int32 [2048, 2], P(('grp', 'node', 'local')), may hold values from 0 to 3, all different within a row; in each aligned block of 64 rows (0 to 63, 64 to 127, ...) at most 40 rows name the same one
- scores: float32 [2048, 2], P(('grp', 'node', 'local')), may hold values from 0.05 to 1
- w_gate: bfloat16 [7168, 8192], P(None, ('node', 'local')), may hold values from -0.0625 to 0.0625
- w_up: bfloat16 [7168, 8192], P(None, ('node', 'local')), may hold values from -0.0625 to 0.0625
- w_down: bfloat16 [32, 2048, 896], P(('node', 'local')), may hold values from -0.125 to 0.125
Outputs:
- mixed: bfloat16 [2048, 7168], P(('grp', 'node', 'local'))
Inputs may be any that keep to these rules, and one draw needn't show every extreme that they name: `expert_ids`: each row names 2 different experts and every expert is named by some row; within the rows of one device no expert is named by more than 40 rows, a bound that some block reaches.
All inputs are finite; a program needn't handle non-finite values.
Results may differ from a plain program's by a relative error of at most 0.0059.
Values may be sent and summed in bfloat16 or wider, within the bound.
A program may use at most 192 MiB of HBM per device.

v0:
```python
import jax
import jax.numpy as jnp
from jax import lax
from jax.sharding import PartitionSpec as P

SPLIT = 8


def swapped(value, axis, stride):
    mask = 2**stride
    pairs = [(source, source ^ mask) for source in range(lax.axis_size(axis))]
    return lax.ppermute(value, axis, pairs)


def on_device(tokens, expert_ids, scores, w_gate, w_up, w_down):
    tok_rows = tokens.shape[0]
    width_model = tokens.shape[1]
    node_count = lax.axis_size("node")
    local_count = lax.axis_size("local")
    device_total = node_count * local_count
    expert_count = device_total // SPLIT
    top_count = expert_ids.shape[1]
    capacity = min(tok_rows, max(2, tok_rows * top_count * 5 // (expert_count * 4)))
    slot_total = expert_count * capacity
    column_width = w_down.shape[2]
    local_index = lax.axis_index("local")
    weights = 2.5 * scores / jnp.sum(scores, axis=1, keepdims=True)
    flat_ids = expert_ids.reshape(-1)
    flat_hot = (flat_ids[:, None] == jnp.arange(expert_count, dtype=jnp.int32)[None, :]).astype(
        jnp.int32
    )
    earlier = jnp.cumsum(flat_hot, axis=0) - flat_hot
    place_in = jnp.sum(earlier * flat_hot, axis=1)
    slot_of = flat_ids * capacity + place_in
    slot_match = (slot_of[:, None] == jnp.arange(slot_total, dtype=jnp.int32)[None, :]).astype(
        jnp.float32
    )
    token_slots = jnp.sum(slot_match.reshape(tok_rows, top_count, slot_total), axis=1)
    slot_weight = jnp.sum(slot_match * weights.reshape(-1)[:, None], axis=0).astype(jnp.bfloat16)
    picked_rows = jnp.dot(
        token_slots.T.astype(jnp.bfloat16), tokens, preferred_element_type=jnp.float32
    ).astype(jnp.bfloat16)
    outgoing_weight = jnp.broadcast_to(
        slot_weight.reshape(expert_count, 1, capacity), (expert_count, SPLIT, capacity)
    )
    outgoing = jnp.broadcast_to(
        picked_rows.reshape(expert_count, 1, capacity, width_model),
        (expert_count, SPLIT, capacity, width_model),
    )
    arrived, arrived_weight = (
        lax.all_to_all(
            outgoing.reshape(device_total, capacity, width_model),
            ("node", "local"),
            split_axis=0,
            concat_axis=0,
            tiled=True,
        ),
        lax.all_to_all(
            outgoing_weight.reshape(device_total, capacity),
            ("node", "local"),
            split_axis=0,
            concat_axis=0,
            tiled=True,
        ),
    )
    row_block = arrived.reshape(device_total * capacity, width_model)
    coefficient = arrived_weight.reshape(device_total * capacity, 1).astype(jnp.float32)
    gate_proj = jnp.dot(row_block, w_gate, preferred_element_type=jnp.float32)
    up_proj = jnp.dot(row_block, w_up, preferred_element_type=jnp.float32)
    hidden = (jax.nn.silu(gate_proj) * up_proj * coefficient).astype(jnp.bfloat16)
    assembled = hidden
    for bit_number in range(SPLIT.bit_length() - 1):
        partner = swapped(assembled, "local", bit_number)
        lower = local_index >> bit_number & 1 == 0
        assembled = jnp.where(
            lower,
            jnp.concatenate([assembled, partner], axis=1),
            jnp.concatenate([partner, assembled], axis=1),
        )
    produced = jnp.dot(assembled, w_down[0], preferred_element_type=jnp.float32)
    returned = lax.all_to_all(
        produced.reshape(device_total, capacity, column_width),
        ("node", "local"),
        split_axis=0,
        concat_axis=0,
        tiled=True,
    )
    returned = returned.reshape(expert_count, SPLIT, capacity, column_width)
    gather_table = token_slots.reshape(tok_rows, expert_count, capacity)
    combined = jnp.einsum("tek,eskd->tsd", gather_table, returned, precision=lax.Precision.HIGHEST)
    return combined.reshape(tok_rows, width_model).astype(jnp.bfloat16)


def solution(mesh):
    placed = (
        P(("grp", "node", "local"), None),
        P(("grp", "node", "local"), None),
        P(("grp", "node", "local"), None),
        P(None, ("node", "local")),
        P(None, ("node", "local")),
        P(("node", "local"), None, None),
    )
    return jax.shard_map(
        on_device,
        mesh=mesh,
        in_specs=placed,
        out_specs=P(("grp", "node", "local"), None),
        check_vma=False,
    )
```

profile of v0, /device:TPU:0, one launch (start us, length us, event | category | flops | bytes accessed | tf_op | source)
XLA Modules:
  0.0 695.2 jit_solution(14893991864927124485)
XLA Ops:
  0.0 0.8 copy.44
  1.4 0.7 reduce_sum.41
  3.9 7.3 %all-to-all-start.1 = ((bf16[32,1,40]{2,1,0:T(2,128)(2,1)}), bf16[32,1,40]{2,1,0:T(2,128)(2,1)S(1)}, u32[]{:S(2)}, u32[]{:S(2)}) async-start(bf16[32,1,40]{2,1,0:T(2,128)(2,1)} %copy.48), calls=%async_computation.1 | async-start | bytes 32768 | tf_op jit(solution)/shard_map/all_to_all | solution.py:58
  12.8 0.8 convolution_convert_fusion
  13.6 4.7 all-to-all-done.1
  18.3 6.5 broadcast_in_dim.7
  24.8 3.9 all-to-all-start
  28.8 408.0 %all-to-all-done = bf16[32,40,7168]{2,1,0:T(8,128)(2,1)} async-done(((bf16[32,40,7168]{2,1,0:T(8,128)(2,1)}), bf16[32,40,7168]{2,1,0:T(8,128)(2,1)}, u32[]{:S(2)}, u32[]{:S(2)}) %all-to-all-start) | async-done | bytes 18350112 | tf_op jit(solution)/shard_map/all_to_all | solution.py:51
  436.8 10.0 %fusion.14 = f32[1280,256]{1,0:T(8,128)S(1)} fusion(bf16[1280,7168]{1,0:T(8,128)(2,1)} %bitcast.3, bf16[7168,256]{1,0:T(8,128)(2,1)} %param.9), kind=kOutput, calls=%fused_computation.33 | convolution fusion | flops 4697620480 | bytes 23330816 | tf_op jit(solution)/shard_map/dot_general | solution.py:68
  446.8 11.4 %fusion.10 = bf16[1280,256]{1,0:T(8,128)(2,1)S(1)} fusion(bf16[1280,7168]{1,0:T(8,128)(2,1)} %bitcast.3, bf16[7168,256]{1,0:T(8,128)(2,1)S(1)} %copy-done.5, f32[1280,256]{1,0:T(8,128)S(1)} %fusion.14, f32[1280]{0:T(1024)S(1)} %reshape.78), kind=kOutput, calls=%fused_computation.16 | convolution fusion | flops 4699914240 | bytes 23991296 | tf_op jit(solution)/shard_map/dot_general | solution.py:69
  458.2 4.2 collective-permute-start
  462.4 15.2 %collective-permute-done = bf16[1280,256]{1,0:T(8,128)(2,1)S(1)} collective-permute-done((bf16[1280,256]{1,0:T(8,128)(2,1)S(1)}, bf16[1280,256]{1,0:T(8,128)(2,1)S(1)}, u32[]{:S(2)}, u32[]{:S(2)}) %collective-permute-start) | collective-permute-done | bytes 655392 | tf_op jit(solution)/shard_map/ppermute | solution.py:12
  477.6 0.8 copy-done.2
  478.8 30.5 %collective-permute-done.1 = bf16[1280,512]{1,0:T(8,128)(2,1)S(1)} collective-permute-done((bf16[1280,512]{1,0:T(8,128)(2,1)S(1)}, bf16[1280,512]{1,0:T(8,128)(2,1)S(1)}, u32[]{:S(2)}, u32[]{:S(2)}) %collective-permute-start.1) | collective-permute-done | bytes 1310752 | tf_op jit(solution)/shard_map/ppermute | solution.py:12
  509.3 1.9 maximum_select_fusion.3
  511.2 1.9 collective-permute-start.2
  513.0 1.6 maximum_select_fusion.4
  514.7 0.8 maximum_select_fusion.2
  515.4 53.7 %collective-permute-done.2 = bf16[1280,1024]{1,0:T(8,128)(2,1)} collective-permute-done((bf16[1280,1024]{1,0:T(8,128)(2,1)}, bf16[1280,1024]{1,0:T(8,128)(2,1)}, u32[]{:S(2)}, u32[]{:S(2)}) %collective-permute-start.2) | collective-permute-done | bytes 2621472 | tf_op jit(solution)/shard_map/ppermute | solution.py:12
  569.2 9.8 %fusion.1 = f32[32,40,896]{2,1,0:T(8,128)} fusion(bf16[32,40,1024]{2,1,0:T(8,128)(2,1)} %bitcast.8, bf16[32,40,1024]{2,1,0:T(8,128)(2,1)S(1)} %maximum_select_fusion.2, pred[]{:T(512)S(6)} %eq.51, bf16[1,2048,896]{2,1,0:T(8,128)(2,1)S(1)} %copy-done.6), kind=kOutput, calls=%fused_computation.4 | convolution fusion | flops 4721213440 | bytes 13500417 | tf_op jit(solution)/shard_map/dot_general | solution.py:80
  579.0 4.9 all-to-all-start.2
  584.0 104.8 %all-to-all-done.2 = f32[32,40,896]{2,1,0:T(8,128)} async-done(((f32[32,40,896]{2,1,0:T(8,128)}), f32[32,40,896]{2,1,0:T(8,128)}, u32[]{:S(2)}, u32[]{:S(2)}) %all-to-all-start.2) | async-done | bytes 4587552 | tf_op jit(solution)/shard_map/all_to_all | solution.py:81
  688.8 2.9 copy.50
  691.7 3.5 fusion
  (34 shorter events, 4.5 us)
Async XLA Ops:
  0.0 12.8 %copy-start = (bf16[64,7168]{1,0:T(8,128)(2,1)S(1)}, bf16[64,7168]{1,0:T(8,128)(2,1)}, u32[]{:S(2)}) copy-start(bf16[64,7168]{1,0:T(8,128)(2,1)} %param.6) | copy-start | bytes 2752516
  3.9 14.4 %all-to-all-start.1 = ((bf16[32,1,40]{2,1,0:T(2,128)(2,1)}), bf16[32,1,40]{2,1,0:T(2,128)(2,1)S(1)}, u32[]{:S(2)}, u32[]{:S(2)}) async-start(bf16[32,1,40]{2,1,0:T(2,128)(2,1)} %copy.48), calls=%async_computation.1 | async-start | bytes 32768 | tf_op jit(solution)/shard_map/all_to_all | solution.py:58
  12.2 0.6 copy-start.3
  24.8 412.0 %all-to-all-start = ((bf16[32,40,7168]{2,1,0:T(8,128)(2,1)}), bf16[32,40,7168]{2,1,0:T(8,128)(2,1)}, u32[]{:S(2)}, u32[]{:S(2)}) async-start(bf16[32,40,7168]{2,1,0:T(8,128)(2,1)} %bitcast.30), calls=%async_computation | async-start | bytes 36700160 | tf_op jit(solution)/shard_map/all_to_all | solution.py:51
  436.8 10.0 %copy-start.5 = (bf16[7168,256]{1,0:T(8,128)(2,1)S(1)}, bf16[7168,256]{1,0:T(8,128)(2,1)}, u32[]{:S(2)}) copy-start(bf16[7168,256]{1,0:T(8,128)(2,1)} %param.10) | copy-start | bytes 11010052
  458.2 19.4 %collective-permute-start = (bf16[1280,256]{1,0:T(8,128)(2,1)S(1)}, bf16[1280,256]{1,0:T(8,128)(2,1)S(1)}, u32[]{:S(2)}, u32[]{:S(2)}) collective-permute-start(bf16[1280,256]{1,0:T(8,128)(2,1)S(1)} %fusion.10), channel_id=1, source_target_pairs={{0,1},{1,0},{2,3},{3,2},{4,5},{5,4},{6,7},{7,6},{8,9},{9,8},{10,11... | collective-permute-start | bytes 1966088 | tf_op jit(solution)/shard_map/ppermute | solution.py:12
  477.6 0.8 copy-start.2
  478.7 30.5 %collective-permute-start.1 = (bf16[1280,512]{1,0:T(8,128)(2,1)S(1)}, bf16[1280,512]{1,0:T(8,128)(2,1)S(1)}, u32[]{:S(2)}, u32[]{:S(2)}) collective-permute-start(bf16[1280,512]{1,0:T(8,128)(2,1)S(1)} %maximum_select_fusion.5), channel_id=1, source_target_pairs={{0,2},{1,3},{2,0},{3,1},{4,6},{5,7},{6,4},{7,5},{8,10},{9,11},{10,... | collective-permute-start | bytes 3932168 | tf_op jit(solution)/shard_map/ppermute | solution.py:12
  511.2 58.0 %collective-permute-start.2 = (bf16[1280,1024]{1,0:T(8,128)(2,1)}, bf16[1280,1024]{1,0:T(8,128)(2,1)}, u32[]{:S(2)}, u32[]{:S(2)}) collective-permute-start(bf16[1280,1024]{1,0:T(8,128)(2,1)} %maximum_select_fusion.3), channel_id=1, source_target_pairs={{0,4},{1,5},{2,6},{3,7},{4,0},{5,1},{6,2},{7,3},{8,12},{9,13},{10,... | collective-permute-start | bytes 7864328 | tf_op jit(solution)/shard_map/ppermute | solution.py:12
  514.6 54.6 %copy-start.6 = (bf16[1,2048,896]{2,1,0:T(8,128)(2,1)S(1)}, bf16[1,2048,896]{2,1,0:T(8,128)(2,1)}, u32[]{:S(2)}) copy-start(bf16[1,2048,896]{2,1,0:T(8,128)(2,1)} %param.11) | copy-start | bytes 11010052
  579.0 4.9 copy-start.4
  579.0 109.8 %all-to-all-start.2 = ((f32[32,40,896]{2,1,0:T(8,128)}), f32[32,40,896]{2,1,0:T(8,128)}, u32[]{:S(2)}, u32[]{:S(2)}) async-start(f32[32,40,896]{2,1,0:T(8,128)} %fusion.1), calls=%async_computation.2 | async-start | bytes 9175040 | tf_op jit(solution)/shard_map/all_to_all | solution.py:81
  691.7 3.5 copy-start.1
where the time goes:
time: 696 us; the launch traced here: 695 us
  waiting for transfers between devices  617 us (89%)
  matrix products  35.4 us (5%)
  starting transfers between devices  22.2 us (3%)
  local copies, waits for them, and re-layouts  13.2 us (2%)
  other arithmetic  7.34 us (1%)
    all_to_all x1, waiting for transfers between devices, on_device(): lax.all_to_all(outgoing.reshape(device_total, capacity, width_model), ('n...  408 us
    all_to_all x1, waiting for transfers between devices, on_device(): lax.all_to_all(produced.reshape(device_total, capacity, column_width), ('...  105 us
    ppermute x3, waiting for transfers between devices, swapped(): return lax.ppermute(value, axis, pairs)  99.4 us
  transfers between devices with their start and end apart: 6, of which 6 were waited for; matrix products, arithmetic and copies ran while one was open for 1% of the time, Pallas kernels for 0%

commit v1 on v0

v1 whole, which is shorter than its diff:
```python
import jax
import jax.numpy as jnp
from jax import lax
from jax.sharding import PartitionSpec as P

SPLIT = 8


def on_device(tokens, expert_ids, scores, w_gate, w_up, w_down):
    rows, width = tokens.shape
    nodes, locals_ = lax.axis_size("node"), lax.axis_size("local")
    devices = nodes * locals_
    experts = devices // SPLIT
    halves = locals_ // SPLIT
    top = expert_ids.shape[1]
    cap = min(rows, max(2, rows * top * 5 // (experts * 4)))
    columns = w_down.shape[2]
    mine = lax.axis_index("node") * halves + lax.axis_index("local") // SPLIT

    weights = 2.5 * scores / jnp.sum(scores, axis=1, keepdims=True)
    hot = expert_ids[:, :, None] == jnp.arange(experts, dtype=jnp.int32)
    route = jnp.sum(jnp.where(hot, weights[:, :, None], 0.0), axis=1)
    route = lax.all_gather(route.astype(jnp.bfloat16), ("node", "local"), axis=0)
    route_mine = lax.dynamic_slice_in_dim(route, mine, 1, 2)[:, :, 0].astype(jnp.float32)
    named = route_mine > 0
    upto = jnp.cumsum(named.astype(jnp.int32), axis=1) - 1
    slot = jnp.where(named, upto, -1)
    pack = (slot[:, None, :] == jnp.arange(cap, dtype=jnp.int32)[None, :, None]).astype(jnp.bfloat16)

    gathered = lax.all_gather(tokens, "local", axis=0, tiled=True)
    gathered = lax.all_gather(gathered, "node", axis=0, tiled=True)
    gate = jnp.dot(gathered, w_gate, preferred_element_type=jnp.float32)
    up = jnp.dot(gathered, w_up, preferred_element_type=jnp.float32)
    hidden = (jax.nn.silu(gate) * up * route_mine.reshape(-1, 1)).astype(jnp.bfloat16)
    packed = jnp.einsum("sct,sth->sch", pack, hidden.reshape(devices, rows, -1),
                        preferred_element_type=jnp.float32).astype(jnp.bfloat16)
    groups = [list(range(h * SPLIT, (h + 1) * SPLIT)) for h in range(halves)]
    whole = lax.all_gather(packed, "local", axis=0, axis_index_groups=groups)
    spread = jnp.einsum("sct,fsch->stfh", pack, whole,
                        preferred_element_type=jnp.float32).astype(jnp.bfloat16)
    out = jnp.dot(spread.reshape(devices * rows, -1), w_down[0], preferred_element_type=jnp.float32)
    half = lax.psum_scatter(out, "node", scatter_dimension=0, tiled=True)
    half = half.astype(jnp.bfloat16).reshape(locals_, rows, columns)
    back = lax.all_to_all(half, "local", split_axis=0, concat_axis=0, tiled=True)
    back = back.astype(jnp.float32).reshape(halves, SPLIT, rows, columns)
    mixed = jnp.sum(back, axis=0)
    return mixed.transpose(1, 0, 2).reshape(rows, width).astype(jnp.bfloat16)


def solution(mesh):
    placed = (
        P(("grp", "node", "local"), None),
        P(("grp", "node", "local"), None),
        P(("grp", "node", "local"), None),
        P(None, ("node", "local")),
        P(None, ("node", "local")),
        P(("node", "local"), None, None),
    )
    return jax.shard_map(
        on_device,
        mesh=mesh,
        in_specs=placed,
        out_specs=P(("grp", "node", "local"), None),
        check_vma=False,
    )
```

time: 696 us -> 511 us (0.73)
  waiting for transfers between devices: 617 us -> 300 us
  blocking collectives: 0 us -> 116 us
  starting transfers between devices: 22.2 us -> 0.3 us
  matrix products: 35.4 us -> 50.2 us
  local copies, waits for them, and re-layouts: 13.2 us -> 27.7 us
  between operations: 0.19 us -> 13.2 us
    all_to_all x3 -> x0, waiting for transfers between devices: 517 us -> none  [the longest x1 408 us: on_device(): lax.all_to_all(outgoing.reshape(device_total, capacity, width_model), ('n...]
    all_gather x0 -> x3, waiting for transfers between devices: none -> 280 us  [the longest x1 177 us: on_device(): gathered = lax.all_gather(tokens, 'local', axis=0, tiled=True)]
    ppermute x3 -> x0, waiting for transfers between devices: 99.4 us -> none  [swapped(): return lax.ppermute(value, axis, pairs)]
    all_gather x0 -> x1, blocking collectives: none -> 65.4 us  [on_device(): lax.all_gather(route.astype(jnp.bfloat16), ('node', 'local'), axis=0)]
    all_to_all x0 -> x1, blocking collectives: none -> 50.9 us  [on_device(): lax.all_to_all(half, 'local', split_axis=0, concat_axis=0, tiled=True)]
    reduce_scatter x0 -> x1, waiting for transfers between devices: none -> 18.7 us  [on_device(): half = lax.psum_scatter(out, 'node', scatter_dimension=0, tiled=True)]
    convert_element_type x2 -> x3, local copies, waits for them, and re-layouts: 0.17 us -> 16.4 us  [the longest x1 15.2 us: on_device(): spread = jnp.einsum('sct,fsch->stfh', pack, whole, preferred_element_type...]
    all_to_all x3 -> x0, starting transfers between devices: 16.1 us -> none  [the longest x1 7.3 us: on_device(): lax.all_to_all(outgoing_weight.reshape(device_total, capacity), ('node',...]
  transfers between devices with their start and end apart: 6 -> 4, of which waited for: 6 -> 3; matrix products, arithmetic and copies ran while one was open for 1% -> 0% of each run, Pallas kernels for 0% -> 0%
where the time goes in v1:
time: 511 us
  waiting for transfers between devices  300 us (59%)
  blocking collectives  116 us (23%)
  matrix products  50.2 us (10%)
  local copies, waits for them, and re-layouts  27.7 us (5%)
  between operations  13.2 us (3%)
    all_gather x1, waiting for transfers between devices, on_device(): gathered = lax.all_gather(tokens, 'local', axis=0, tiled=True)  177 us
    all_gather x1, waiting for transfers between devices, on_device(): whole = lax.all_gather(packed, 'local', axis=0, axis_index_groups=groups)  103 us
    all_gather x1, blocking collectives, on_device(): lax.all_gather(route.astype(jnp.bfloat16), ('node', 'local'), axis=0)  65.4 us
    all_to_all x1, blocking collectives, on_device(): lax.all_to_all(half, 'local', split_axis=0, concat_axis=0, tiled=True)  50.9 us
    reduce_scatter x1, waiting for transfers between devices, on_device(): half = lax.psum_scatter(out, 'node', scatter_dimension=0, tiled=True)  18.7 us
    convert_element_type x1, local copies, waits for them, and re-layouts, on_device(): spread = jnp.einsum('sct,fsch->stfh', pack, whole, preferred_element_type...  15.2 us
    dot_general x1, matrix products, on_device(): gate = jnp.dot(gathered, w_gate, preferred_element_type=jnp.float32)  14.5 us
    dot_general x1, matrix products, on_device(): up = jnp.dot(gathered, w_up, preferred_element_type=jnp.float32)  13.4 us
  transfers between devices with their start and end apart: 4, of which 3 were waited for; matrix products, arithmetic and copies ran while one was open for 0% of the time, Pallas kernels for 0%

profile of v1, /device:TPU:0, one launch (start us, length us, event | category | flops | bytes accessed | tf_op | source)
XLA Modules:
  0.0 510.8 jit_solution(10400316030553704845)
XLA Ops:
  6.5 0.7 all-gather.7.cloned.1.call-update
  7.3 0.0 all-gather.9.cloned.1.call-start
  7.3 177.4 %all-gather.7.cloned.1.call-done = bf16[1024,7168]{1,0:T(8,128)(2,1)} async-done(((bf16[64,7168]{1,0:T(8,128)(2,1)}), bf16[1024,7168]{1,0:T(8,128)(2,1)}) %all-gather.7.cloned.1.call-update) | async-done | bytes 14680080 | tf_op jit(solution)/shard_map/all_gather | solution.py:30
  184.7 0.0 all-gather.9.cloned.1.call-update
  184.8 0.0 all-gather.11.cloned.1.call-start
  184.8 0.6 copy-done
  185.5 65.4 %all-gather.2 = bf16[32,64,4]{1,2,0:T(4,128)(2,1)S(1)} all-gather(bf16[1,64,4]{1,2,0:T(4,128)(2,1)S(1)} %bitcast.39), channel_id=2, replica_groups=mesh['grp'=1,'node'=2,'local'=16] {'node','local'}, dimensions={0}, use_global_device_ids=true | all-gather | bytes 16896 | tf_op jit(solution)/shard_map/all_gather | solution.py:23
  250.9 0.1 reshape.64
  251.0 0.2 reduce_window_sum.11
  251.2 14.5 %fusion.9 = f32[2048,256]{1,0:T(8,128)S(1)} fusion(bf16[2048,7168]{1,0:T(8,128)(2,1)} %all-gather.9.cloned.1.call-done, bf16[7168,256]{1,0:T(8,128)(2,1)} %param.9), kind=kOutput, calls=%fused_computation.21 | convolution fusion | flops 7516192768 | bytes 35127296 | tf_op jit(solution)/shard_map/dot_general | solution.py:32
  265.8 13.4 %fusion.4 = bf16[2048,256]{1,0:T(8,128)(2,1)S(1)} fusion(bf16[2048,7168]{1,0:T(8,128)(2,1)} %all-gather.9.cloned.1.call-done, bf16[7168,256]{1,0:T(8,128)(2,1)S(1)} %copy-done.2, f32[2048,256]{1,0:T(8,128)S(1)} %fusion.9, f32[2048]{0:T(1024)S(1)} %reshape.64), kind=kOutput, calls=%fused_computation.6 | convolution fusion | flops 7519862784 | bytes 36184064 | tf_op jit(solution)/shard_map/dot_general | solution.py:33
  279.1 1.2 convolution_convert_fusion.1
  280.3 0.0 all-gather.11.cloned.1.call-update
  280.3 0.2 reduce-scatter.2.cloned.1.call-start
  280.6 102.9 %all-gather.11.cloned.1.call-done = bf16[256,40,256]{2,1,0:T(8,128)(2,1)} async-done(((bf16[32,40,256]{2,1,0:T(8,128)(2,1)}), bf16[256,40,256]{2,1,0:T(8,128)(2,1)}) %all-gather.11.cloned.1.call-update) | async-done | bytes 5242896 | tf_op jit(solution)/shard_map/all_gather | solution.py:38
  383.5 8.1 %convolution_convert_fusion = bf16[32,64,8,256]{3,1,2,0:T(8,128)(2,1)} fusion(bf16[8,32,40,256]{3,2,1,0:T(8,128)(2,1)} %bitcast.36, s32[32,64]{1,0:T(8,128)S(1)} %add_select_fusion), kind=kOutput, calls=%fused_computation | convolution fusion | flops 339820544 | bytes 13639680 | tf_op jit(solution)/shard_map/sct,fsch->stfh/dot_general | solution.py:39
  391.6 15.2 %copy.27 = bf16[32,64,8,256]{3,2,1,0:T(8,128)(2,1)} copy(bf16[32,64,8,256]{3,1,2,0:T(8,128)(2,1)} %convolution_convert_fusion) | data formatting | bytes 16777216 | tf_op jit(solution)/shard_map/convert_element_type | solution.py:40
  406.8 10.7 %copy.32 = bf16[256,8,8,256]{3,1,2,0:T(8,128)(2,1)} copy(bf16[256,8,8,256]{3,2,1,0:T(8,128)(2,1)} %bitcast.32) | data formatting | bytes 16777216
  417.5 13.0 %fusion.1 = f32[2048,896]{1,0:T(8,128)} fusion(bf16[2048,2048]{1,0:T(8,128)(2,1)} %bitcast.33, bf16[1,2048,896]{2,1,0:T(8,128)(2,1)S(1)} %copy-done.3), kind=kOutput, calls=%fused_computation.2 | convolution fusion | flops 7516192768 | bytes 19398656 | tf_op jit(solution)/shard_map/dot_general | solution.py:41
  430.5 18.7 %reduce-scatter.2.cloned.1.call-done = f32[1024,896]{1,0:T(8,128)} async-done(((f32[2048,896]{1,0:T(8,128)}), f32[1024,896]{1,0:T(8,128)}) %reduce-scatter.2.cloned.1.call-update) | async-done | bytes 3670032 | tf_op jit(solution)/shard_map/reduce_scatter | solution.py:42
  449.2 2.2 convert_element_type.73
  451.5 50.9 %all_to_all.5 = bf16[16,64,896]{2,1,0:T(8,128)(2,1)S(1)} all-to-all(bf16[16,64,896]{2,1,0:T(8,128)(2,1)S(1)} %bitcast.35), channel_id=1, replica_groups=mesh['grp'=1,'node'=2,'local'=16] {'local'}, dimensions={0} | all-to-all | bytes 3670016 | tf_op jit(solution)/shard_map/all_to_all | solution.py:44
  502.4 0.8 reduce
  503.2 1.1 copy.31
  (17 shorter events, 0.1 us)
Async XLA Ops:
  6.5 178.2 %all-gather.7.cloned.1.call-start = ((), (), s32[]{:S(2)}) async-start(), calls=%async_computation.2 | async-start | bytes 15597568 | tf_op jit(solution)/shard_map/all_gather | solution.py:30
  7.3 244.0 %all-gather.9.cloned.1.call-start = ((), (), s32[]{:S(2)}) async-start(), calls=%async_computation.3 | async-start | bytes 44040192 | tf_op jit(solution)/shard_map/all_gather | solution.py:31
  184.7 0.7 copy-start
  184.7 0.7 copy-start.1
  184.8 198.7 %all-gather.11.cloned.1.call-start = ((), (), s32[]{:S(2)}) async-start(), calls=%async_computation.5 | async-start | bytes 5898240 | tf_op jit(solution)/shard_map/all_gather | solution.py:38
  251.2 14.5 %copy-start.2 = (bf16[7168,256]{1,0:T(8,128)(2,1)S(1)}, bf16[7168,256]{1,0:T(8,128)(2,1)}, u32[]{:S(2)}) copy-start(bf16[7168,256]{1,0:T(8,128)(2,1)} %param.10) | copy-start | bytes 11010052
  280.3 168.9 %reduce-scatter.2.cloned.1.call-start = ((), (), s32[]{:S(2)}) async-start(), calls=%async_computation.4 | async-start | bytes 11010048 | tf_op jit(solution)/shard_map/reduce_scatter | solution.py:42
  406.8 10.7 %copy-start.3 = (bf16[1,2048,896]{2,1,0:T(8,128)(2,1)S(1)}, bf16[1,2048,896]{2,1,0:T(8,128)(2,1)}, u32[]{:S(2)}) copy-start(bf16[1,2048,896]{2,1,0:T(8,128)(2,1)} %param.11) | copy-start | bytes 11010052
Sparse Core Ops, SparseCore 0:
  10.1 174.5 all-gather.6
  186.3 45.0 all-gather.8
  280.5 102.9 all-gather.10
  430.7 18.5 reduce-scatter.1

commit v2 on v1

--- a/solution.py
+++ b/solution.py
@@ -1,9 +1,235 @@
 import jax
 import jax.numpy as jnp
 from jax import lax
+from jax.experimental import pallas as pl
+from jax.experimental.pallas import tpu as pltpu
 from jax.sharding import PartitionSpec as P
 
 SPLIT = 8
+MESH = pl.DeviceIdType.MESH
+
+
+def device(core, local):
+    return {"node": core, "local": local}
+
+
+def token_gather(lines, own_ref, all_ref, send_sem, recv_sem, own_sem):
+    core, local = lax.axis_index("node"), lax.axis_index("local")
+    count = lines * 4
+    z, y, x = local // 4, local // 2 % 2, local % 2
+    to_x, to_y = local + 1 - 2 * x, local + 2 - 4 * y
+    first = (1 - core) * to_x + core * to_y
+    second = core * to_x + (1 - core) * to_y
+    below, above = local - 4, local + 4
+    base, other = core * count, (1 - core) * count
+
+    place = pltpu.make_async_copy(own_ref, all_ref.at[base + local], own_sem)
+    place.start()
+    barrier = pltpu.get_barrier_semaphore()
+    for peer in (device(core, first), device(core, second), device(1 - core, local)):
+        pl.semaphore_signal(barrier, inc=1, device_id=peer, device_id_type=MESH)
+
+    @pl.when(z > 0)
+    def _():
+        pl.semaphore_signal(barrier, inc=1, device_id=device(core, below), device_id_type=MESH)
+
+    @pl.when(z < lines - 1)
+    def _():
+        pl.semaphore_signal(barrier, inc=1, device_id=device(core, above), device_id_type=MESH)
+
+    ends = (z + lines - 2) // (lines - 1) + (2 * lines - 3 - z) // (lines - 1)
+    pl.semaphore_wait(barrier, 3 + ends)
+    place.wait()
+
+    def copy(source, kind, peer):
+        return pltpu.make_async_remote_copy(
+            src_ref=all_ref.at[base + source],
+            dst_ref=all_ref.at[base + source],
+            send_sem=send_sem.at[source, kind],
+            recv_sem=recv_sem.at[base + source],
+            device_id=peer,
+            device_id_type=MESH,
+        )
+
+    def arrived(slot):
+        pltpu.make_async_remote_copy(
+            src_ref=all_ref.at[slot],
+            dst_ref=all_ref.at[slot],
+            send_sem=send_sem.at[0, 0],
+            recv_sem=recv_sem.at[slot],
+            device_id=device(1 - core, local),
+            device_id_type=MESH,
+        ).wait_recv()
+
+    def up(source):
+        return copy(source, 0, device(core, above))
+
+    def down(source):
+        return copy(source, 1, device(core, below))
+
+    def to_second(source):
+        return copy(source, 2, device(core, second))
+
+    def to_first(source):
+        return copy(source, 3, device(core, first))
+
+    def to_core(source):
+        return copy(source, 4, device(1 - core, local))
+
+    def when(fits, action):
+        @pl.when(fits)
+        def _():
+            action()
+
+    def line(run):
+        for step in range(lines):
+            for sign in (-1, 1) if step else (0,):
+                shift = sign * step
+                fits = jnp.logical_and(z + shift >= 0, z + shift < lines)
+                when(fits, lambda shift=shift, sign=sign: run(shift * 4, sign))
+
+    def pass_on(shift, sign):
+        source = local + shift
+        if sign:
+            arrived(base + source)
+        if sign <= 0:
+            when(z < lines - 1, lambda: up(source).start())
+        if sign >= 0:
+            when(z > 0, lambda: down(source).start())
+        to_first(source).start()
+        to_second(source).start()
+        to_core(source).start()
+
+    def pass_first(shift, sign):
+        source = first + shift
+        arrived(base + source)
+        to_second(source).start()
+        to_core(source).start()
+
+    def pass_second(shift, sign, start):
+        source = start + shift
+        arrived(base + source)
+        to_core(source).start()
+
+    opposite = first + second - local
+    steps = []
+    for step in range(lines):
+        for sign in (-1, 1) if step else (0,):
+            steps.append((step, sign))
+    for at in range(len(steps) + 2):
+        for lag, run in (
+            (0, pass_on),
+            (1, pass_first),
+            (2, lambda a, b: (pass_second(a, b, second), pass_second(a, b, opposite))),
+        ):
+            if 0 <= at - lag < len(steps):
+                step, sign = steps[at - lag]
+                shift = step * sign
+                fits = jnp.logical_and(z + shift >= 0, z + shift < lines)
+                when(fits, lambda run=run, shift=shift, sign=sign: run(shift * 4, sign))
+    for source in range(count):
+        arrived(other + source)
+
+    def sent(shift, sign):
+        source = local + shift
+        if sign <= 0:
+            when(z < lines - 1, lambda: up(source).wait_send())
+        if sign >= 0:
+            when(z > 0, lambda: down(source).wait_send())
+        to_first(source).wait_send()
+        to_second(source).wait_send()
+        to_second(first + shift).wait_send()
+
+    line(sent)
+    for source in range(count):
+        to_core(source).wait_send()
+
+
+def hidden_gather(own_ref, all_ref, send_sem, recv_sem, own_sem):
+    core, local = lax.axis_index("node"), lax.axis_index("local")
+    rows, width = own_ref.shape
+    third = -(-rows // 48) * 16
+    cuts = [(0, third), (third, third), (2 * third, rows - 2 * third)]
+    within = local % SPLIT
+    flips = [(1 - 2 * (local // stride % 2)) * stride for stride in (1, 2, 4)]
+
+    def block(index):
+        return pl.ds(pl.multiple_of(index * width, width), width)
+
+    place = pltpu.make_async_copy(own_ref, all_ref.at[:, block(within)], own_sem)
+    place.start()
+    barrier = pltpu.get_barrier_semaphore()
+    for flip in flips:
+        pl.semaphore_signal(barrier, inc=1, device_id=device(core, local + flip), device_id_type=MESH)
+    pl.semaphore_wait(barrier, len(flips))
+    place.wait()
+
+    def copy(part, source, axis, peer):
+        start, size = cuts[part]
+        here = all_ref.at[pl.ds(start, size), block(source)]
+        return pltpu.make_async_remote_copy(
+            src_ref=here,
+            dst_ref=here,
+            send_sem=send_sem.at[part, axis, source],
+            recv_sem=recv_sem.at[part, source],
+            device_id=device(core, peer),
+            device_id_type=MESH,
+        )
+
+    pending = []
+
+    def send(part, source, axes):
+        for axis in axes:
+            moved = copy(part, source, axis, local + flips[axis])
+            moved.start()
+            pending.append(moved)
+
+    orders = [[(part + turn) % 3 for turn in range(3)] for part in range(3)]
+    held = [[within] for _ in range(3)]
+    for part, order in enumerate(orders):
+        send(part, within, order)
+    for turn in range(3):
+        for place_in in range(2**turn):
+            for part, order in enumerate(orders):
+                source = held[part][place_in] + flips[order[turn]]
+                copy(part, source, 0, local + flips[order[turn]]).wait_recv()
+                send(part, source, order[turn + 1 :])
+                held[part].append(source)
+    for moved in pending:
+        moved.wait_send()
+
+
+def gather_tokens(tokens, lines):
+    rows, width = tokens.shape
+    count = lines * 4
+    return pl.pallas_call(
+        lambda *refs: token_gather(lines, *refs),
+        out_shape=jax.ShapeDtypeStruct((2 * count, rows, width), tokens.dtype),
+        in_specs=[pl.BlockSpec(memory_space=pl.ANY)],
+        out_specs=pl.BlockSpec(memory_space=pl.ANY),
+        scratch_shapes=[
+            pltpu.SemaphoreType.DMA((count, 5)),
+            pltpu.SemaphoreType.DMA((2 * count,)),
+            pltpu.SemaphoreType.DMA,
+        ],
+        compiler_params=pltpu.CompilerParams(collective_id=0, has_side_effects=True),
+    )(tokens)
+
+
+def gather_hidden(packed):
+    rows, width = packed.shape
+    return pl.pallas_call(
+        hidden_gather,
+        out_shape=jax.ShapeDtypeStruct((rows, SPLIT * width), packed.dtype),
+        in_specs=[pl.BlockSpec(memory_space=pl.ANY)],
+        out_specs=pl.BlockSpec(memory_space=pl.ANY),
+        scratch_shapes=[
+            pltpu.SemaphoreType.DMA((3, 3, SPLIT)),
+            pltpu.SemaphoreType.DMA((3, SPLIT)),
+            pltpu.SemaphoreType.DMA,
+        ],
+        compiler_params=pltpu.CompilerParams(collective_id=1, has_side_effects=True),
+    )(packed)
 
 
 def on_device(tokens, expert_ids, scores, w_gate, w_up, w_down):
@@ -27,18 +253,27 @@
     slot = jnp.where(named, upto, -1)
     pack = (slot[:, None, :] == jnp.arange(cap, dtype=jnp.int32)[None, :, None]).astype(jnp.bfloat16)
 
-    gathered = lax.all_gather(tokens, "local", axis=0, tiled=True)
-    gathered = lax.all_gather(gathered, "node", axis=0, tiled=True)
+    boxed = nodes == 2 and locals_ == 2 * SPLIT
+    if boxed:
+        gathered = gather_tokens(tokens, locals_ // 4).reshape(devices * rows, width)
+    else:
+        gathered = lax.all_gather(tokens, "local", axis=0, tiled=True)
+        gathered = lax.all_gather(gathered, "node", axis=0, tiled=True)
     gate = jnp.dot(gathered, w_gate, preferred_element_type=jnp.float32)
     up = jnp.dot(gathered, w_up, preferred_element_type=jnp.float32)
     hidden = (jax.nn.silu(gate) * up * route_mine.reshape(-1, 1)).astype(jnp.bfloat16)
     packed = jnp.einsum("sct,sth->sch", pack, hidden.reshape(devices, rows, -1),
                         preferred_element_type=jnp.float32).astype(jnp.bfloat16)
-    groups = [list(range(h * SPLIT, (h + 1) * SPLIT)) for h in range(halves)]
-    whole = lax.all_gather(packed, "local", axis=0, axis_index_groups=groups)
-    spread = jnp.einsum("sct,fsch->stfh", pack, whole,
-                        preferred_element_type=jnp.float32).astype(jnp.bfloat16)
-    out = jnp.dot(spread.reshape(devices * rows, -1), w_down[0], preferred_element_type=jnp.float32)
+    packed = packed.reshape(devices * cap, -1)
+    if boxed:
+        whole = gather_hidden(packed)
+    else:
+        groups = [list(range(h * SPLIT, (h + 1) * SPLIT)) for h in range(halves)]
+        whole = lax.all_gather(packed, "local", axis=1, axis_index_groups=groups, tiled=True)
+    out = jnp.dot(whole, w_down[0], preferred_element_type=jnp.float32).astype(jnp.bfloat16)
+    out = jnp.einsum("sct,scd->std", pack, out.reshape(devices, cap, columns),
+                     preferred_element_type=jnp.float32).astype(jnp.bfloat16)
+    out = out.reshape(devices * rows, columns)
     half = lax.psum_scatter(out, "node", scatter_dimension=0, tiled=True)
     half = half.astype(jnp.bfloat16).reshape(locals_, rows, columns)
     back = lax.all_to_all(half, "local", split_axis=0, concat_axis=0, tiled=True)

time: 511 us -> 415 us (0.81)
  waiting for transfers between devices: 300 us -> 11.8 us
  Pallas kernels: 0 us -> 223 us
  local copies, waits for them, and re-layouts: 27.7 us -> 1.15 us
  matrix products: 50.2 us -> 40.6 us
    all_gather x3 -> x0, waiting for transfers between devices: 280 us -> none  [the longest x1 177 us: on_device(): gathered = lax.all_gather(tokens, 'local', axis=0, tiled=True)]
    pallas_call x0 -> x2, Pallas kernels: none -> 223 us  [the longest x1 167 us: gather_tokens(): pl.pallas_call(lambda *refs: token_gather(lines, *refs), out_shape=jax.Sh...]
    convert_element_type x1 -> x0, local copies, waits for them, and re-layouts: 15.2 us -> none  [on_device(): spread = jnp.einsum('sct,fsch->stfh', pack, whole, preferred_element_type...]
    unnamed x9 -> x2, local copies, waits for them, and re-layouts: 11.3 us -> 0.01 us
    dot_general x2, matrix products: 21.1 us -> 11.6 us  [the longest x1 8.61 us: on_device(): jnp.dot(whole, w_down[0], preferred_element_type=jnp.float32)]
    reduce_scatter x1, waiting for transfers between devices: 18.7 us -> 11.8 us  [on_device(): half = lax.psum_scatter(out, 'node', scatter_dimension=0, tiled=True)]
  transfers between devices with their start and end apart: 4 -> 1, of which waited for: 3 -> 1; matrix products, arithmetic and copies ran while one was open for 0% -> 0% of each run, Pallas kernels for 0% -> 0%
where the time goes in v2:
time: 415 us; the launch traced here: 414 us
  Pallas kernels  223 us (54%)
  blocking collectives  121 us (29%)
  matrix products  40.6 us (10%)
  between operations  13.5 us (3%)
  waiting for transfers between devices  11.8 us (3%)
    pallas_call x1, Pallas kernels, gather_tokens(): pl.pallas_call(lambda *refs: token_gather(lines, *refs), out_shape=jax.Sh...  167 us
    all_gather x1, blocking collectives, on_device(): lax.all_gather(route.astype(jnp.bfloat16), ('node', 'local'), axis=0)  70 us
    pallas_call x1, Pallas kernels, gather_hidden(): pl.pallas_call(hidden_gather, out_shape=jax.ShapeDtypeStruct((rows, SPLIT...  56 us
    all_to_all x1, blocking collectives, on_device(): lax.all_to_all(half, 'local', split_axis=0, concat_axis=0, tiled=True)  51 us
    dot_general x1, matrix products, on_device(): gate = jnp.dot(gathered, w_gate, preferred_element_type=jnp.float32)  14.5 us
    dot_general x1, matrix products, on_device(): up = jnp.dot(gathered, w_up, preferred_element_type=jnp.float32)  13.4 us
    reduce_scatter x1, waiting for transfers between devices, on_device(): half = lax.psum_scatter(out, 'node', scatter_dimension=0, tiled=True)  11.8 us
    dot_general x1, matrix products, on_device(): jnp.dot(whole, w_down[0], preferred_element_type=jnp.float32)  8.61 us
  transfers between devices with their start and end apart: 1, of which 1 were waited for; matrix products, arithmetic and copies ran while one was open for 0% of the time, Pallas kernels for 0%

profile of v2, /device:TPU:0, one launch (start us, length us, event | category | flops | bytes accessed | tf_op | source)
XLA Modules:
  0.0 414.3 jit_solution(16542896621077897774)
XLA Ops:
  6.5 0.0 reduce-scatter.2.cloned.1.call-start
  6.5 0.7 reduce_sum.27
  7.2 0.7 multiply_divide_fusion
  7.9 0.7 select_reduce_fusion
  8.6 70.0 %all-gather.1 = bf16[32,64,4]{1,2,0:T(4,128)(2,1)S(1)} all-gather(bf16[1,64,4]{1,2,0:T(4,128)(2,1)S(1)} %bitcast.39), channel_id=2, replica_groups=mesh['grp'=1,'node'=2,'local'=16] {'node','local'}, dimensions={0}, use_global_device_ids=true | all-gather | bytes 16896 | tf_op jit(solution)/shard_map/all_gather | solution.py:249
  78.7 0.1 reshape.76
  78.7 0.2 reduce_window_sum.11
  79.0 167.1 %shard_map.64 = bf16[32,64,7168]{2,1,0:T(8,128)(2,1)} custom-call(bf16[64,7168]{1,0:T(8,128)(2,1)} %refs_0_.1), custom_call_target="tpu_custom_call" | custom-call | tf_op jit(solution)/shard_map/pallas_call | solution.py:205
  246.0 0.0 copy-start
  246.0 14.5 %fusion.9 = f32[2048,256]{1,0:T(8,128)S(1)} fusion(bf16[2048,7168]{1,0:T(8,128)(2,1)} %bitcast.30, bf16[7168,256]{1,0:T(8,128)(2,1)} %param.9), kind=kOutput, calls=%fused_computation.20 | convolution fusion | flops 7516192768 | bytes 35127296 | tf_op jit(solution)/shard_map/dot_general | solution.py:262
  260.6 0.0 copy-done
  260.6 13.4 %fusion.6 = bf16[2048,256]{1,0:T(8,128)(2,1)S(1)} fusion(bf16[2048,7168]{1,0:T(8,128)(2,1)} %bitcast.31, bf16[7168,256]{1,0:T(8,128)(2,1)S(1)} %copy-done, f32[2048,256]{1,0:T(8,128)S(1)} %fusion.9, f32[2048]{0:T(1024)S(1)} %reshape.76), kind=kOutput, calls=%fused_computation.5 | convolution fusion | flops 7519862784 | bytes 36184064 | tf_op jit(solution)/shard_map/dot_general | solution.py:263
  274.0 1.2 convolution_convert_fusion.1
  275.1 56.0 %shard_map.65 = bf16[1280,2048]{1,0:T(8,128)(2,1)} custom-call(bf16[1280,256]{1,0:T(8,128)(2,1)} %bitcast.35), custom_call_target="tpu_custom_call" | custom-call | tf_op jit(solution)/shard_map/pallas_call | solution.py:221
  331.2 8.6 %fusion.2 = bf16[1280,896]{1,0:T(8,128)(2,1)S(1)} fusion(bf16[1280,2048]{1,0:T(8,128)(2,1)} %shard_map.65, bf16[1,2048,896]{2,1,0:T(8,128)(2,1)} %param.11), kind=kOutput, calls=%fused_computation.2 | convolution fusion | flops 4698767360 | bytes 11206656 | tf_op jit(solution)/shard_map/dot_general | solution.py:273
  339.8 3.0 convolution_convert_fusion
  342.8 0.0 reduce-scatter.2.cloned.1.call-update
  342.8 11.8 %reduce-scatter.2.cloned.1.call-done = bf16[1024,896]{1,0:T(8,128)(2,1)} async-done(((bf16[2048,896]{1,0:T(8,128)(2,1)}), bf16[1024,896]{1,0:T(8,128)(2,1)}) %reduce-scatter.2.cloned.1.call-update) | async-done | bytes 1835024 | tf_op jit(solution)/shard_map/reduce_scatter | solution.py:277
  354.6 51.0 %all_to_all.5 = bf16[16,64,896]{2,1,0:T(8,128)(2,1)S(1)} all-to-all(bf16[16,64,896]{2,1,0:T(8,128)(2,1)} %bitcast.37), channel_id=1, replica_groups=mesh['grp'=1,'node'=2,'local'=16] {'local'}, dimensions={0} | all-to-all | bytes 3670016 | tf_op jit(solution)/shard_map/all_to_all | solution.py:279
  405.6 0.8 reduce
  406.4 1.1 copy.22
  (4 shorter events, 0.0 us)
Async XLA Ops:
  6.5 348.1 %reduce-scatter.2.cloned.1.call-start = ((), (), s32[]{:S(2)}) async-start(), calls=%async_computation.2 | async-start | bytes 5505024 | tf_op jit(solution)/shard_map/reduce_scatter | solution.py:277
  246.0 14.5 %copy-start = (bf16[7168,256]{1,0:T(8,128)(2,1)S(1)}, bf16[7168,256]{1,0:T(8,128)(2,1)}, u32[]{:S(2)}) copy-start(bf16[7168,256]{1,0:T(8,128)(2,1)} %param.10) | copy-start | bytes 11010052
Sparse Core Ops, SparseCore 0:
  342.9 11.6 reduce-scatter.1

commit v3 on v2

--- a/solution.py
+++ b/solution.py
@@ -13,7 +13,20 @@
     return {"node": core, "local": local}
 
 
-def token_gather(lines, own_ref, all_ref, send_sem, recv_sem, own_sem):
+class Copies:
+    def __init__(self, make, count):
+        self.make = make
+        self.count = count
+
+    def start(self, at):
+        self.make(at).start()
+
+    def wait_send(self):
+        for at in range(self.count):
+            self.make(at).wait_send()
+
+
+def token_gather(lines, own_ref, note_ref, all_ref, notes_ref, send_sem, recv_sem, own_sem):
     core, local = lax.axis_index("node"), lax.axis_index("local")
     count = lines * 4
     z, y, x = local // 4, local // 2 % 2, local % 2
@@ -23,8 +36,11 @@
     below, above = local - 4, local + 4
     base, other = core * count, (1 - core) * count
 
-    place = pltpu.make_async_copy(own_ref, all_ref.at[base + local], own_sem)
+    half = own_ref.shape[0] // 2
+    place = pltpu.make_async_copy(own_ref, all_ref.at[base + local], own_sem.at[0])
     place.start()
+    place_note = pltpu.make_async_copy(note_ref, notes_ref.at[base + local], own_sem.at[1])
+    place_note.start()
     barrier = pltpu.get_barrier_semaphore()
     for peer in (device(core, first), device(core, second), device(1 - core, local)):
         pl.semaphore_signal(barrier, inc=1, device_id=peer, device_id_type=MESH)
@@ -40,23 +56,36 @@
     ends = (z + lines - 2) // (lines - 1) + (2 * lines - 3 - z) // (lines - 1)
     pl.semaphore_wait(barrier, 3 + ends)
     place.wait()
+    place_note.wait()
+
+    def views(slot):
+        return (
+            all_ref.at[slot, pl.ds(0, half)],
+            all_ref.at[slot, pl.ds(half, half)],
+            notes_ref.at[slot],
+        )
 
     def copy(source, kind, peer):
-        return pltpu.make_async_remote_copy(
-            src_ref=all_ref.at[base + source],
-            dst_ref=all_ref.at[base + source],
-            send_sem=send_sem.at[source, kind],
-            recv_sem=recv_sem.at[base + source],
-            device_id=peer,
-            device_id_type=MESH,
-        )
-
-    def arrived(slot):
+        def make(at):
+            view = views(base + source)[at]
+            return pltpu.make_async_remote_copy(
+                src_ref=view,
+                dst_ref=view,
+                send_sem=send_sem.at[source, kind, at],
+                recv_sem=recv_sem.at[base + source, at],
+                device_id=peer,
+                device_id_type=MESH,
+            )
+
+        return Copies(make, 3)
+
+    def arrived(slot, at):
+        view = views(slot)[at]
         pltpu.make_async_remote_copy(
-            src_ref=all_ref.at[slot],
-            dst_ref=all_ref.at[slot],
-            send_sem=send_sem.at[0, 0],
-            recv_sem=recv_sem.at[slot],
+            src_ref=view,
+            dst_ref=view,
+            send_sem=send_sem.at[0, 0, at],
+            recv_sem=recv_sem.at[slot, at],
             device_id=device(1 - core, local),
             device_id_type=MESH,
         ).wait_recv()
@@ -90,26 +119,29 @@
 
     def pass_on(shift, sign):
         source = local + shift
-        if sign:
-            arrived(base + source)
-        if sign <= 0:
-            when(z < lines - 1, lambda: up(source).start())
-        if sign >= 0:
-            when(z > 0, lambda: down(source).start())
-        to_first(source).start()
-        to_second(source).start()
-        to_core(source).start()
+        for at in range(3):
+            if sign:
+                arrived(base + source, at)
+            if sign <= 0:
+                when(z < lines - 1, lambda: up(source).start(at))
+            if sign >= 0:
+                when(z > 0, lambda: down(source).start(at))
+            to_second(source).start(at)
+            to_first(source).start(at)
+            to_core(source).start(at)
 
     def pass_first(shift, sign):
         source = first + shift
-        arrived(base + source)
-        to_second(source).start()
-        to_core(source).start()
+        for at in range(3):
+            arrived(base + source, at)
+            to_second(source).start(at)
+            to_core(source).start(at)
 
     def pass_second(shift, sign, start):
         source = start + shift
-        arrived(base + source)
-        to_core(source).start()
+        for at in range(3):
+            arrived(base + source, at)
+            to_core(source).start(at)
 
     opposite = first + second - local
     steps = []
@@ -128,7 +160,8 @@
                 fits = jnp.logical_and(z + shift >= 0, z + shift < lines)
                 when(fits, lambda run=run, shift=shift, sign=sign: run(shift * 4, sign))
     for source in range(count):
-        arrived(other + source)
+        for at in range(3):
+            arrived(other + source, at)
 
     def sent(shift, sign):
         source = local + shift
@@ -199,21 +232,24 @@
         moved.wait_send()
 
 
-def gather_tokens(tokens, lines):
+def gather_tokens(tokens, note, lines):
     rows, width = tokens.shape
     count = lines * 4
     return pl.pallas_call(
         lambda *refs: token_gather(lines, *refs),
-        out_shape=jax.ShapeDtypeStruct((2 * count, rows, width), tokens.dtype),
-        in_specs=[pl.BlockSpec(memory_space=pl.ANY)],
-        out_specs=pl.BlockSpec(memory_space=pl.ANY),
+        out_shape=(
+            jax.ShapeDtypeStruct((2 * count, rows, width), tokens.dtype),
+            jax.ShapeDtypeStruct((2 * count,) + note.shape, note.dtype),
+        ),
+        in_specs=[pl.BlockSpec(memory_space=pl.ANY)] * 2,
+        out_specs=(pl.BlockSpec(memory_space=pl.ANY),) * 2,
         scratch_shapes=[
-            pltpu.SemaphoreType.DMA((count, 5)),
-            pltpu.SemaphoreType.DMA((2 * count,)),
-            pltpu.SemaphoreType.DMA,
+            pltpu.SemaphoreType.DMA((count, 5, 3)),
+            pltpu.SemaphoreType.DMA((2 * count, 3)),
+            pltpu.SemaphoreType.DMA((2,)),
         ],
         compiler_params=pltpu.CompilerParams(collective_id=0, has_side_effects=True),
-    )(tokens)
+    )(tokens, note)
 
 
 def gather_hidden(packed):
@@ -246,19 +282,23 @@
     weights = 2.5 * scores / jnp.sum(scores, axis=1, keepdims=True)
     hot = expert_ids[:, :, None] == jnp.arange(experts, dtype=jnp.int32)
     route = jnp.sum(jnp.where(hot, weights[:, :, None], 0.0), axis=1)
-    route = lax.all_gather(route.astype(jnp.bfloat16), ("node", "local"), axis=0)
+    route = route.astype(jnp.bfloat16)
+    boxed = nodes == 2 and locals_ == 2 * SPLIT and experts <= 16 and rows <= 128 and rows % 32 == 0
+    if boxed:
+        note = jnp.pad(route.T, ((0, 16 - experts), (0, 128 - rows)))
+        gathered, notes = gather_tokens(tokens, note, locals_ // 4)
+        gathered = gathered.reshape(devices * rows, width)
+        route = notes[:, :experts, :rows].transpose(0, 2, 1)
+    else:
+        gathered = lax.all_gather(tokens, "local", axis=0, tiled=True)
+        gathered = lax.all_gather(gathered, "node", axis=0, tiled=True)
+        route = lax.all_gather(route, ("node", "local"), axis=0)
     route_mine = lax.dynamic_slice_in_dim(route, mine, 1, 2)[:, :, 0].astype(jnp.float32)
     named = route_mine > 0
     upto = jnp.cumsum(named.astype(jnp.int32), axis=1) - 1
     slot = jnp.where(named, upto, -1)
     pack = (slot[:, None, :] == jnp.arange(cap, dtype=jnp.int32)[None, :, None]).astype(jnp.bfloat16)
 
-    boxed = nodes == 2 and locals_ == 2 * SPLIT
-    if boxed:
-        gathered = gather_tokens(tokens, locals_ // 4).reshape(devices * rows, width)
-    else:
-        gathered = lax.all_gather(tokens, "local", axis=0, tiled=True)
-        gathered = lax.all_gather(gathered, "node", axis=0, tiled=True)
     gate = jnp.dot(gathered, w_gate, preferred_element_type=jnp.float32)
     up = jnp.dot(gathered, w_up, preferred_element_type=jnp.float32)
     hidden = (jax.nn.silu(gate) * up * route_mine.reshape(-1, 1)).astype(jnp.bfloat16)

time: 415 us -> 339 us (0.82)
  blocking collectives: 121 us -> 51 us
  Pallas kernels: 223 us -> 218 us
    all_gather x1 -> x0, blocking collectives: 70 us -> none  [on_device(): lax.all_gather(route.astype(jnp.bfloat16), ('node', 'local'), axis=0)]
    pallas_call x1, Pallas kernels: 167 us -> 162 us  [gather_tokens(): pl.pallas_call(lambda *refs: token_gather(lines, *refs), out_shape=(jax.S...]
where the time goes in v3:
time: 339 us
  Pallas kernels  218 us (64%)
  blocking collectives  51 us (15%)
  matrix products  40.6 us (12%)
  between operations  13.5 us (4%)
  waiting for transfers between devices  9.8 us (3%)
    pallas_call x1, Pallas kernels, gather_tokens(): pl.pallas_call(lambda *refs: token_gather(lines, *refs), out_shape=(jax.S...  162 us
    pallas_call x1, Pallas kernels, gather_hidden(): pl.pallas_call(hidden_gather, out_shape=jax.ShapeDtypeStruct((rows, SPLIT...  56.5 us
    all_to_all x1, blocking collectives, on_device(): lax.all_to_all(half, 'local', split_axis=0, concat_axis=0, tiled=True)  51 us
    dot_general x1, matrix products, on_device(): gate = jnp.dot(gathered, w_gate, preferred_element_type=jnp.float32)  14.5 us
    dot_general x1, matrix products, on_device(): up = jnp.dot(gathered, w_up, preferred_element_type=jnp.float32)  13.4 us
    reduce_scatter x1, waiting for transfers between devices, on_device(): half = lax.psum_scatter(out, 'node', scatter_dimension=0, tiled=True)  9.79 us
    dot_general x1, matrix products, on_device(): jnp.dot(whole, w_down[0], preferred_element_type=jnp.float32)  8.61 us
  transfers between devices with their start and end apart: 1, of which 1 were waited for; matrix products, arithmetic and copies ran while one was open for 0% of the time, Pallas kernels for 0%

profile of v3, /device:TPU:0, one launch (start us, length us, event | category | flops | bytes accessed | tf_op | source)
XLA Modules:
  0.0 339.1 jit_solution(11527499384537134040)
XLA Ops:
  6.5 0.0 reduce-scatter.2.cloned.1.call-start
  6.5 0.7 reduce_sum.27
  7.2 0.7 multiply_divide_fusion
  7.9 0.7 select_reduce_fusion
  8.6 0.6 pad.4.refs_1_
  9.2 161.8 %shard_map.64 = (bf16[32,64,7168]{2,1,0:T(8,128)(2,1)}, bf16[32,16,128]{2,1,0:T(8,128)(2,1)}) custom-call(bf16[64,7168]{1,0:T(8,128)(2,1)} %refs_0_.1, bf16[16,128]{1,0:T(8,128)(2,1)} %pad.4.refs_1_), custom_call_target="tpu_custom_call" | custom-call | tf_op jit(solution)/shard_map/pallas_call | solution.py:238
  171.0 0.9 slice.3
  171.9 0.1 convert_reduce_fusion
  172.0 0.1 reshape.58
  172.1 0.2 reduce_window_sum.11
  172.4 0.0 copy-start
  172.4 14.5 %fusion.9 = f32[2048,256]{1,0:T(8,128)S(1)} fusion(bf16[2048,7168]{1,0:T(8,128)(2,1)} %bitcast.40, bf16[7168,256]{1,0:T(8,128)(2,1)} %param.9), kind=kOutput, calls=%fused_computation.19 | convolution fusion | flops 7516192768 | bytes 35127296 | tf_op jit(solution)/shard_map/dot_general | solution.py:302
  186.9 0.0 copy-done
  186.9 13.4 %fusion.6 = bf16[2048,256]{1,0:T(8,128)(2,1)S(1)} fusion(bf16[2048,7168]{1,0:T(8,128)(2,1)} %bitcast.41, bf16[7168,256]{1,0:T(8,128)(2,1)S(1)} %copy-done, f32[2048,256]{1,0:T(8,128)S(1)} %fusion.9, f32[2048]{0:T(1024)S(1)} %reshape.58), kind=kOutput, calls=%fused_computation.5 | convolution fusion | flops 7519862784 | bytes 36184064 | tf_op jit(solution)/shard_map/dot_general | solution.py:303
  200.3 1.2 convolution_convert_fusion.1
  201.5 56.5 %shard_map.65 = bf16[1280,2048]{1,0:T(8,128)(2,1)} custom-call(bf16[1280,256]{1,0:T(8,128)(2,1)} %bitcast.31), custom_call_target="tpu_custom_call" | custom-call | tf_op jit(solution)/shard_map/pallas_call | solution.py:257
  258.0 8.6 %fusion.2 = bf16[1280,896]{1,0:T(8,128)(2,1)S(1)} fusion(bf16[1280,2048]{1,0:T(8,128)(2,1)} %shard_map.65, bf16[1,2048,896]{2,1,0:T(8,128)(2,1)} %param.11), kind=kOutput, calls=%fused_computation.2 | convolution fusion | flops 4698767360 | bytes 11206656 | tf_op jit(solution)/shard_map/dot_general | solution.py:313
  266.6 3.0 convolution_convert_fusion
  269.6 0.0 reduce-scatter.2.cloned.1.call-update
  269.6 9.8 %reduce-scatter.2.cloned.1.call-done = bf16[1024,896]{1,0:T(8,128)(2,1)} async-done(((bf16[2048,896]{1,0:T(8,128)(2,1)}), bf16[1024,896]{1,0:T(8,128)(2,1)}) %reduce-scatter.2.cloned.1.call-update) | async-done | bytes 1835024 | tf_op jit(solution)/shard_map/reduce_scatter | solution.py:317
  279.4 51.0 %all_to_all.5 = bf16[16,64,896]{2,1,0:T(8,128)(2,1)S(1)} all-to-all(bf16[16,64,896]{2,1,0:T(8,128)(2,1)} %bitcast.33), channel_id=1, replica_groups=mesh['grp'=1,'node'=2,'local'=16] {'local'}, dimensions={0} | all-to-all | bytes 3670016 | tf_op jit(solution)/shard_map/all_to_all | solution.py:319
  330.4 0.8 reduce
  331.2 1.1 copy.27
  (5 shorter events, 0.1 us)
Async XLA Ops:
  6.5 272.9 %reduce-scatter.2.cloned.1.call-start = ((), (), s32[]{:S(2)}) async-start(), calls=%async_computation.2 | async-start | bytes 5505024 | tf_op jit(solution)/shard_map/reduce_scatter | solution.py:317
  172.4 14.5 %copy-start = (bf16[7168,256]{1,0:T(8,128)(2,1)S(1)}, bf16[7168,256]{1,0:T(8,128)(2,1)}, u32[]{:S(2)}) copy-start(bf16[7168,256]{1,0:T(8,128)(2,1)} %param.10) | copy-start | bytes 11010052
Sparse Core Ops, SparseCore 0:
  269.7 9.6 reduce-scatter.1

commit v4 on v3

--- a/solution.py
+++ b/solution.py
@@ -14,15 +14,14 @@
 
 
 class Copies:
-    def __init__(self, make, count):
+    def __init__(self, make):
         self.make = make
-        self.count = count
 
     def start(self, at):
         self.make(at).start()
 
-    def wait_send(self):
-        for at in range(self.count):
+    def wait_send(self, pieces):
+        for at in pieces:
             self.make(at).wait_send()
 
 
@@ -36,7 +35,7 @@
     below, above = local - 4, local + 4
     base, other = core * count, (1 - core) * count
 
-    half = own_ref.shape[0] // 2
+    quarter = own_ref.shape[0] // 4
     place = pltpu.make_async_copy(own_ref, all_ref.at[base + local], own_sem.at[0])
     place.start()
     place_note = pltpu.make_async_copy(note_ref, notes_ref.at[base + local], own_sem.at[1])
@@ -60,9 +59,10 @@
 
     def views(slot):
         return (
-            all_ref.at[slot, pl.ds(0, half)],
-            all_ref.at[slot, pl.ds(half, half)],
+            all_ref.at[slot, pl.ds(0, 2 * quarter)],
+            all_ref.at[slot, pl.ds(2 * quarter, quarter)],
             notes_ref.at[slot],
+            all_ref.at[slot, pl.ds(3 * quarter, quarter)],
         )
 
     def copy(source, kind, peer):
@@ -77,7 +77,7 @@
                 device_id_type=MESH,
             )
 
-        return Copies(make, 3)
+        return Copies(make)
 
     def arrived(slot, at):
         view = views(slot)[at]
@@ -144,6 +144,30 @@
             to_core(source).start(at)
 
     opposite = first + second - local
+    plane = (local, first, second, opposite)
+
+    def plane_step(at):
+        for source in ((local,), (first,), (second, opposite))[at]:
+            if at:
+                arrived(base + source, 3)
+            if at == 0:
+                to_first(source).start(3)
+            if at <= 1:
+                to_second(source).start(3)
+            when(z < lines - 1, lambda source=source: up(source).start(3))
+            when(z > 0, lambda source=source: down(source).start(3))
+            to_core(source).start(3)
+
+    def along(shift, sign):
+        for start in plane:
+            source = start + shift
+            arrived(base + source, 3)
+            if sign < 0:
+                when(z < lines - 1, lambda source=source: up(source).start(3))
+            else:
+                when(z > 0, lambda source=source: down(source).start(3))
+            to_core(source).start(3)
+
     steps = []
     for step in range(lines):
         for sign in (-1, 1) if step else (0,):
@@ -159,23 +183,38 @@
                 shift = step * sign
                 fits = jnp.logical_and(z + shift >= 0, z + shift < lines)
                 when(fits, lambda run=run, shift=shift, sign=sign: run(shift * 4, sign))
+        if at < 3:
+            plane_step(at)
+        elif at - 2 < len(steps):
+            step, sign = steps[at - 2]
+            shift = step * sign
+            fits = jnp.logical_and(z + shift >= 0, z + shift < lines)
+            when(fits, lambda shift=shift, sign=sign: along(shift * 4, sign))
     for source in range(count):
-        for at in range(3):
+        for at in range(4):
             arrived(other + source, at)
 
     def sent(shift, sign):
         source = local + shift
         if sign <= 0:
-            when(z < lines - 1, lambda: up(source).wait_send())
+            when(z < lines - 1, lambda: up(source).wait_send(range(4)))
         if sign >= 0:
-            when(z > 0, lambda: down(source).wait_send())
-        to_first(source).wait_send()
-        to_second(source).wait_send()
-        to_second(first + shift).wait_send()
+            when(z > 0, lambda: down(source).wait_send(range(4)))
+        to_first(source).wait_send(range(3))
+        to_second(source).wait_send(range(3))
+        to_second(first + shift).wait_send(range(3))
+        for start in plane[1:]:
+            if sign <= 0:
+                when(z < lines - 1, lambda start=start: up(start + shift).wait_send([3]))
+            if sign >= 0:
+                when(z > 0, lambda start=start: down(start + shift).wait_send([3]))
 
     line(sent)
+    to_first(local).wait_send([3])
+    to_second(local).wait_send([3])
+    to_second(first).wait_send([3])
     for source in range(count):
-        to_core(source).wait_send()
+        to_core(source).wait_send(range(4))
 
 
 def hidden_gather(own_ref, all_ref, send_sem, recv_sem, own_sem):
@@ -244,12 +283,40 @@
         in_specs=[pl.BlockSpec(memory_space=pl.ANY)] * 2,
         out_specs=(pl.BlockSpec(memory_space=pl.ANY),) * 2,
         scratch_shapes=[
-            pltpu.SemaphoreType.DMA((count, 5, 3)),
-            pltpu.SemaphoreType.DMA((2 * count, 3)),
+            pltpu.SemaphoreType.DMA((count, 5, 4)),
+            pltpu.SemaphoreType.DMA((2 * count, 4)),
             pltpu.SemaphoreType.DMA((2,)),
         ],
         compiler_params=pltpu.CompilerParams(collective_id=0, has_side_effects=True),
     )(tokens, note)
+
+
+def gated(rows_ref, scale_ref, gate_ref, up_ref, out_ref):
+    gate = jnp.dot(rows_ref[...], gate_ref[...], preferred_element_type=jnp.float32)
+    up = jnp.dot(rows_ref[...], up_ref[...], preferred_element_type=jnp.float32)
+    out_ref[...] = (gate / (1.0 + jnp.exp(-gate)) * up * scale_ref[...]).astype(out_ref.dtype)
+
+
+def expert_hidden(gathered, scale, w_gate, w_up):
+    total, width = gathered.shape
+    units = w_gate.shape[1]
+    tile = 256
+    return pl.pallas_call(
+        gated,
+        out_shape=jax.ShapeDtypeStruct((total, units), jnp.bfloat16),
+        grid=(total // tile,),
+        in_specs=[
+            pl.BlockSpec((tile, width), lambda i: (i, 0)),
+            pl.BlockSpec((tile, 1), lambda i: (i, 0)),
+            pl.BlockSpec((width, units), lambda i: (0, 0)),
+            pl.BlockSpec((width, units), lambda i: (0, 0)),
+        ],
+        out_specs=pl.BlockSpec((tile, units), lambda i: (i, 0)),
+        compiler_params=pltpu.CompilerParams(vmem_limit_bytes=40 * 2**20),
+        cost_estimate=pl.CostEstimate(
+            flops=4 * total * width * units, bytes_accessed=2 * total * width, transcendentals=total * units
+        ),
+    )(gathered, scale, w_gate, w_up)
 
 
 def gather_hidden(packed):
@@ -283,7 +350,7 @@
     hot = expert_ids[:, :, None] == jnp.arange(experts, dtype=jnp.int32)
     route = jnp.sum(jnp.where(hot, weights[:, :, None], 0.0), axis=1)
     route = route.astype(jnp.bfloat16)
-    boxed = nodes == 2 and locals_ == 2 * SPLIT and experts <= 16 and rows <= 128 and rows % 32 == 0
+    boxed = nodes == 2 and locals_ == 2 * SPLIT and experts <= 16 and rows <= 128 and rows % 64 == 0
     if boxed:
         note = jnp.pad(route.T, ((0, 16 - experts), (0, 128 - rows)))
         gathered, notes = gather_tokens(tokens, note, locals_ // 4)
@@ -299,9 +366,7 @@
     slot = jnp.where(named, upto, -1)
     pack = (slot[:, None, :] == jnp.arange(cap, dtype=jnp.int32)[None, :, None]).astype(jnp.bfloat16)
 
-    gate = jnp.dot(gathered, w_gate, preferred_element_type=jnp.float32)
-    up = jnp.dot(gathered, w_up, preferred_element_type=jnp.float32)
-    hidden = (jax.nn.silu(gate) * up * route_mine.reshape(-1, 1)).astype(jnp.bfloat16)
+    hidden = expert_hidden(gathered, route_mine.reshape(-1, 1), w_gate, w_up)
     packed = jnp.einsum("sct,sth->sch", pack, hidden.reshape(devices, rows, -1),
                         preferred_element_type=jnp.float32).astype(jnp.bfloat16)
     packed = packed.reshape(devices * cap, -1)

time: 339 us -> 337 us (level)
  matrix products: 40.6 us -> 12.8 us
  Pallas kernels: 218 us -> 238 us
  local copies, waits for them, and re-layouts: 2.59 us -> 7.59 us
    dot_general x2 -> x0, matrix products: 27.9 us -> none  [the longest x1 14.5 us: on_device(): gate = jnp.dot(gathered, w_gate, preferred_element_type=jnp.float32)]
    pallas_call x0 -> x1, Pallas kernels: none -> 18.8 us  [expert_hidden(): pl.pallas_call(gated, out_shape=jax.ShapeDtypeStruct((total, units), jnp....]
    unnamed x2 -> x4, local copies, waits for them, and re-layouts: 0.01 us -> 4.07 us
where the time goes in v4:
time: 337 us; the launch traced here: 336 us
  Pallas kernels  238 us (71%)
  blocking collectives  51 us (15%)
  between operations  13.5 us (4%)
  matrix products  12.8 us (4%)
  waiting for transfers between devices  10.1 us (3%)
  local copies, waits for them, and re-layouts  7.59 us (2%)
    pallas_call x1, Pallas kernels, gather_tokens(): pl.pallas_call(lambda *refs: token_gather(lines, *refs), out_shape=(jax.S...  162 us
    pallas_call x1, Pallas kernels, gather_hidden(): pl.pallas_call(hidden_gather, out_shape=jax.ShapeDtypeStruct((rows, SPLIT...  57 us
    all_to_all x1, blocking collectives, on_device(): lax.all_to_all(half, 'local', split_axis=0, concat_axis=0, tiled=True)  51 us
    pallas_call x1, Pallas kernels, expert_hidden(): pl.pallas_call(gated, out_shape=jax.ShapeDtypeStruct((total, units), jnp....  18.8 us
    reduce_scatter x1, waiting for transfers between devices, on_device(): half = lax.psum_scatter(out, 'node', scatter_dimension=0, tiled=True)  10.1 us
    dot_general x1, matrix products, on_device(): jnp.dot(whole, w_down[0], preferred_element_type=jnp.float32)  8.61 us
  transfers between devices with their start and end apart: 1, of which 1 were waited for; matrix products, arithmetic and copies ran while one was open for 0% of the time, Pallas kernels for 0%

profile of v4, /device:TPU:0, one launch (start us, length us, event | category | flops | bytes accessed | tf_op | source)
XLA Modules:
  0.0 336.3 jit_solution(11470936420938040056)
XLA Ops:
  6.5 0.0 reduce-scatter.2.cloned.1.call-start
  6.5 0.7 reduce_sum.27
  7.2 0.7 multiply_divide_fusion
  7.9 0.7 select_reduce_fusion
  8.6 0.6 pad.4.refs_1_
  9.2 162.2 %shard_map.64 = (bf16[32,64,7168]{2,1,0:T(8,128)(2,1)}, bf16[32,16,128]{2,1,0:T(8,128)(2,1)}) custom-call(bf16[64,7168]{1,0:T(8,128)(2,1)} %refs_0_.1, bf16[16,128]{1,0:T(8,128)(2,1)} %pad.4.refs_1_), custom_call_target="tpu_custom_call" | custom-call | tf_op jit(solution)/shard_map/pallas_call | solution.py:277
  171.5 0.9 slice.3
  172.3 0.1 convert_reduce_fusion
  172.5 0.2 reduce_window_sum.11
  172.7 1.0 reshape.64.scale_ref
  173.8 0.0 copy-start
  173.8 2.0 copy-done
  175.8 0.0 copy-start.1
  175.8 2.0 copy-done.1
  177.8 18.8 %shard_map.65 = bf16[2048,256]{1,0:T(8,128)(2,1)S(1)} custom-call(bf16[2048,7168]{1,0:T(8,128)(2,1)} %bitcast.36, f32[2048,1]{1,0:T(8,128)S(1)} %reshape.64.scale_ref, bf16[7168,256]{1,0:T(8,128)(2,1)S(1)} %copy-done, bf16[7168,256]{1,0:T(8,128)(2,1)S(1)} %copy-done.1), custom_call_target="tpu_custom_call" | custom-call | flops 15032385536 | bytes 29360128 | tf_op jit(solution)/shard_map/pallas_call | solution.py:304
  196.6 1.2 convolution_convert_fusion.1
  197.8 57.0 %shard_map.66 = bf16[1280,2048]{1,0:T(8,128)(2,1)} custom-call(bf16[1280,256]{1,0:T(8,128)(2,1)} %bitcast.28), custom_call_target="tpu_custom_call" | custom-call | tf_op jit(solution)/shard_map/pallas_call | solution.py:324
  254.8 8.6 %fusion.2 = bf16[1280,896]{1,0:T(8,128)(2,1)S(1)} fusion(bf16[1280,2048]{1,0:T(8,128)(2,1)} %shard_map.66, bf16[1,2048,896]{2,1,0:T(8,128)(2,1)} %param.11), kind=kOutput, calls=%fused_computation.2 | convolution fusion | flops 4698767360 | bytes 11206656 | tf_op jit(solution)/shard_map/dot_general | solution.py:378
  263.4 3.0 convolution_convert_fusion
  266.4 0.0 reduce-scatter.2.cloned.1.call-update
  266.4 10.1 %reduce-scatter.2.cloned.1.call-done = bf16[1024,896]{1,0:T(8,128)(2,1)} async-done(((bf16[2048,896]{1,0:T(8,128)(2,1)}), bf16[1024,896]{1,0:T(8,128)(2,1)}) %reduce-scatter.2.cloned.1.call-update) | async-done | bytes 1835024 | tf_op jit(solution)/shard_map/reduce_scatter | solution.py:382
  276.6 51.0 %all_to_all.5 = bf16[16,64,896]{2,1,0:T(8,128)(2,1)S(1)} all-to-all(bf16[16,64,896]{2,1,0:T(8,128)(2,1)} %bitcast.30), channel_id=1, replica_groups=mesh['grp'=1,'node'=2,'local'=16] {'local'}, dimensions={0} | all-to-all | bytes 3670016 | tf_op jit(solution)/shard_map/all_to_all | solution.py:384
  327.6 0.8 reduce
  328.4 1.1 copy.36
  (5 shorter events, 0.1 us)
Async XLA Ops:
  6.5 270.0 %reduce-scatter.2.cloned.1.call-start = ((), (), s32[]{:S(2)}) async-start(), calls=%async_computation.2 | async-start | bytes 5505024 | tf_op jit(solution)/shard_map/reduce_scatter | solution.py:382
  173.8 2.0 copy-start
  175.8 2.0 copy-start.1
Sparse Core Ops, SparseCore 0:
  266.6 9.9 reduce-scatter.1

commit v5 on v4

--- a/solution.py
+++ b/solution.py
@@ -225,10 +225,7 @@
     within = local % SPLIT
     flips = [(1 - 2 * (local // stride % 2)) * stride for stride in (1, 2, 4)]
 
-    def block(index):
-        return pl.ds(pl.multiple_of(index * width, width), width)
-
-    place = pltpu.make_async_copy(own_ref, all_ref.at[:, block(within)], own_sem)
+    place = pltpu.make_async_copy(own_ref, all_ref.at[within], own_sem)
     place.start()
     barrier = pltpu.get_barrier_semaphore()
     for flip in flips:
@@ -238,7 +235,7 @@
 
     def copy(part, source, axis, peer):
         start, size = cuts[part]
-        here = all_ref.at[pl.ds(start, size), block(source)]
+        here = all_ref.at[source, pl.ds(start, size)]
         return pltpu.make_async_remote_copy(
             src_ref=here,
             dst_ref=here,
@@ -269,6 +266,32 @@
                 held[part].append(source)
     for moved in pending:
         moved.wait_send()
+
+
+def down(parts_ref, weight_ref, out_ref):
+    parts, _, width = parts_ref.shape
+    rows = jnp.concatenate([parts_ref[part] for part in range(parts)], axis=1)
+    out_ref[...] = jnp.dot(rows, weight_ref[...], preferred_element_type=jnp.float32).astype(out_ref.dtype)
+
+
+def expert_out(parts, weight):
+    count, total, width = parts.shape
+    columns = weight.shape[1]
+    tile = 256
+    return pl.pallas_call(
+        down,
+        out_shape=jax.ShapeDtypeStruct((total, columns), jnp.bfloat16),
+        grid=(pl.cdiv(total, tile),),
+        in_specs=[
+            pl.BlockSpec((count, tile, width), lambda i: (0, i, 0)),
+            pl.BlockSpec((count * width, columns), lambda i: (0, 0)),
+        ],
+        out_specs=pl.BlockSpec((tile, columns), lambda i: (i, 0)),
+        compiler_params=pltpu.CompilerParams(vmem_limit_bytes=32 * 2**20),
+        cost_estimate=pl.CostEstimate(
+            flops=2 * total * count * width * columns, bytes_accessed=4 * total * columns, transcendentals=0
+        ),
+    )(parts, weight)
 
 
 def gather_tokens(tokens, note, lines):
@@ -323,7 +346,7 @@
     rows, width = packed.shape
     return pl.pallas_call(
         hidden_gather,
-        out_shape=jax.ShapeDtypeStruct((rows, SPLIT * width), packed.dtype),
+        out_shape=jax.ShapeDtypeStruct((SPLIT, rows, width), packed.dtype),
         in_specs=[pl.BlockSpec(memory_space=pl.ANY)],
         out_specs=pl.BlockSpec(memory_space=pl.ANY),
         scratch_shapes=[
@@ -371,11 +394,11 @@
                         preferred_element_type=jnp.float32).astype(jnp.bfloat16)
     packed = packed.reshape(devices * cap, -1)
     if boxed:
-        whole = gather_hidden(packed)
+        out = expert_out(gather_hidden(packed), w_down[0])
     else:
         groups = [list(range(h * SPLIT, (h + 1) * SPLIT)) for h in range(halves)]
         whole = lax.all_gather(packed, "local", axis=1, axis_index_groups=groups, tiled=True)
-    out = jnp.dot(whole, w_down[0], preferred_element_type=jnp.float32).astype(jnp.bfloat16)
+        out = jnp.dot(whole, w_down[0], preferred_element_type=jnp.float32).astype(jnp.bfloat16)
     out = jnp.einsum("sct,scd->std", pack, out.reshape(devices, cap, columns),
                      preferred_element_type=jnp.float32).astype(jnp.bfloat16)
     out = out.reshape(devices * rows, columns)

time: 337 us -> 339 us (level)
  matrix products: 12.8 us -> 4.13 us
  Pallas kernels: 238 us -> 245 us
  local copies, waits for them, and re-layouts: 7.59 us -> 12.1 us
    dot_general x1 -> x0, matrix products: 8.61 us -> none  [on_device(): jnp.dot(whole, w_down[0], preferred_element_type=jnp.float32)]
    pallas_call x1 -> x2, Pallas kernels: 57 us -> 63.7 us  [the longest x1 57 us: gather_hidden(): pl.pallas_call(hidden_gather, out_shape=jax.ShapeDtypeStruct((SPLIT, rows...]
    unnamed x4 -> x8, local copies, waits for them, and re-layouts: 4.07 us -> 8.59 us
where the time goes in v5:
time: 339 us
  Pallas kernels  245 us (72%)
  blocking collectives  51 us (15%)
  between operations  13.5 us (4%)
  local copies, waits for them, and re-layouts  12.1 us (4%)
  waiting for transfers between devices  10.1 us (3%)
  matrix products  4.13 us (1%)
    pallas_call x1, Pallas kernels, gather_tokens(): pl.pallas_call(lambda *refs: token_gather(lines, *refs), out_shape=(jax.S...  162 us
    pallas_call x1, Pallas kernels, gather_hidden(): pl.pallas_call(hidden_gather, out_shape=jax.ShapeDtypeStruct((SPLIT, rows...  57 us
    all_to_all x1, blocking collectives, on_device(): lax.all_to_all(half, 'local', split_axis=0, concat_axis=0, tiled=True)  51 us
    pallas_call x1, Pallas kernels, expert_hidden(): pl.pallas_call(gated, out_shape=jax.ShapeDtypeStruct((total, units), jnp....  18.8 us
    reduce_scatter x1, waiting for transfers between devices, on_device(): half = lax.psum_scatter(out, 'node', scatter_dimension=0, tiled=True)  10.1 us
    unnamed x8, local copies, waits for them, and re-layouts  8.59 us
  transfers between devices with their start and end apart: 1, of which 1 were waited for; matrix products, arithmetic and copies ran while one was open for 0% of the time, Pallas kernels for 0%

profile of v5, /device:TPU:0, one launch (start us, length us, event | category | flops | bytes accessed | tf_op | source)
XLA Modules:
  0.0 338.9 jit_solution(444458989943990490)
XLA Ops:
  6.5 0.7 reduce_sum.27
  7.2 0.7 multiply_divide_fusion
  7.9 0.7 select_reduce_fusion
  8.6 0.6 pad.4.refs_1_
  9.2 162.2 %shard_map.64 = (bf16[32,64,7168]{2,1,0:T(8,128)(2,1)}, bf16[32,16,128]{2,1,0:T(8,128)(2,1)}) custom-call(bf16[64,7168]{1,0:T(8,128)(2,1)} %refs_0_.1, bf16[16,128]{1,0:T(8,128)(2,1)} %pad.4.refs_1_), custom_call_target="tpu_custom_call" | custom-call | tf_op jit(solution)/shard_map/pallas_call | solution.py:300
  171.5 0.9 slice.3
  172.3 0.1 convert_reduce_fusion
  172.5 0.2 reduce_window_sum.11
  172.7 1.0 reshape.64.scale_ref
  173.8 0.0 copy-start.1
  173.8 2.0 copy-done.1
  175.8 2.0 copy-done.2
  177.8 18.8 %shard_map.65 = bf16[2048,256]{1,0:T(8,128)(2,1)S(1)} custom-call(bf16[2048,7168]{1,0:T(8,128)(2,1)} %bitcast.32, f32[2048,1]{1,0:T(8,128)S(1)} %reshape.64.scale_ref, bf16[7168,256]{1,0:T(8,128)(2,1)S(1)} %copy-done.1, bf16[7168,256]{1,0:T(8,128)(2,1)S(1)} %copy-done.2), custom_call_target="tpu_custom_call" | custom-call | flops 15032385536 | bytes 29360128 | tf_op jit(solution)/shard_map/pallas_call | solution.py:327
  196.6 1.2 convolution_convert_fusion.1
  197.8 57.0 %shard_map.66.parts_ref = bf16[8,1280,256]{2,1,0:T(8,128)(2,1)} custom-call(bf16[1280,256]{1,0:T(8,128)(2,1)} %bitcast.25), custom_call_target="tpu_custom_call" | custom-call | tf_op jit(solution)/shard_map/pallas_call | solution.py:347
  254.8 2.5 copy-done
  257.3 2.0 copy-done.3
  259.3 6.7 %shard_map.67 = bf16[1280,896]{1,0:T(8,128)(2,1)S(1)} custom-call(bf16[8,1280,256]{2,1,0:T(8,128)(2,1)S(1)} %copy-done, bf16[2048,896]{1,0:T(8,128)(2,1)S(1)} %bitcast.21), custom_call_target="tpu_custom_call" | custom-call | flops 4697620480 | bytes 4587520 | tf_op jit(solution)/shard_map/pallas_call | solution.py:281
  266.0 3.0 convolution_convert_fusion
  269.0 0.0 reduce-scatter.2.cloned.1.call-update
  269.0 10.1 %reduce-scatter.2.cloned.1.call-done = bf16[1024,896]{1,0:T(8,128)(2,1)} async-done(((bf16[2048,896]{1,0:T(8,128)(2,1)}), bf16[1024,896]{1,0:T(8,128)(2,1)}) %reduce-scatter.2.cloned.1.call-update) | async-done | bytes 1835024 | tf_op jit(solution)/shard_map/reduce_scatter | solution.py:405
  279.1 51.0 %all_to_all.5 = bf16[16,64,896]{2,1,0:T(8,128)(2,1)S(1)} all-to-all(bf16[16,64,896]{2,1,0:T(8,128)(2,1)} %bitcast.26), channel_id=1, replica_groups=mesh['grp'=1,'node'=2,'local'=16] {'local'}, dimensions={0} | all-to-all | bytes 3670016 | tf_op jit(solution)/shard_map/all_to_all | solution.py:407
  330.1 0.8 reduce
  331.0 1.1 copy.36
  (9 shorter events, 0.1 us)
Async XLA Ops:
  6.5 272.6 %reduce-scatter.2.cloned.1.call-start = ((), (), s32[]{:S(2)}) async-start(), calls=%async_computation.2 | async-start | bytes 5505024 | tf_op jit(solution)/shard_map/reduce_scatter | solution.py:405
  173.8 2.0 copy-start.1
  175.8 2.0 copy-start.2
  254.8 2.5 copy-start
  257.3 2.0 copy-start.3
Sparse Core Ops, SparseCore 0:
  269.1 9.9 reduce-scatter.1
